TPU v7x, 512 devices: a whole 4x8x8 slice. The times are simulated.
512 devices in a mesh: section: 4 (over x), seq: 128 (over z, y, core).
Axes of the slice: x: 4, y: 8, z: 8, core: 2. Of those that a mesh axis runs over, the one named last changes fastest.
Arguments:
- hidden: bfloat16 [65536, 4096], P('seq', 'section'), may hold values from -6 to 6
- norm_gain: bfloat16 [4096], P('section'), may hold values from 0.25 to 1.75
- query_weight: bfloat16 [4096, 512], P(None, 'section')
- key_weight: bfloat16 [4096, 128], P('section')
- value_weight: bfloat16 [4096, 128], P('section'), may hold values from -0.5 to 0.5
- output_weight: bfloat16 [512, 4096], P(None, 'section'), may hold values from -0.25 to 0.25
- block_reach: int32 [512], P('seq'), may hold values from 0 to 2
- header_ids: int32 [2], replicated, may hold values from 0 to 511, as said below
Outputs:
- attention_out: bfloat16 [65536, 4096], P('seq', 'section')
Inputs may be any that keep to these rules, and one draw needn't show every extreme that they name: `header_ids`: the 2 indices are distinct block indices, and the last block, 511, is always one of them, at any position.
All inputs are finite; a program needn't handle non-finite values.
Results may differ from a plain program's by a relative error of at most 0.014.
Values may be sent and summed in bfloat16 or wider, within the bound.
No kernel may reach another device: no remote copies, remote signals or barrier semaphores. Data moves between devices by JAX's collectives and lax.ppermute only.
A program may use at most 64 MiB of HBM per device.

v0:
```python
import math
import jax
import jax.numpy as jnp
from jax import lax
from jax.sharding import PartitionSpec as P

BLOCK = 128
REACH = 2
EPSILON = 1e-05
THETA = 500000.0


def merged(value, axis, combine):
    everything = jax.tree.map(lambda part: lax.all_gather(part, axis), value)
    leading = jax.tree.map(lambda part: part[0], everything)

    def lap(k, so_far):
        return combine(so_far, jax.tree.map(lambda part: part[k], everything))

    return lax.fori_loop(1, lax.axis_size(axis), lap, leading)


def padded(cells, sides, width):
    for axis, dim in sides:
        count = lax.axis_size(axis)
        ends = count - 1
        head = lax.slice_in_dim(cells, 0, width, axis=dim)
        tail = lax.slice_in_dim(cells, cells.shape[dim] - width, cells.shape[dim], axis=dim)
        cells = jnp.concatenate(
            [
                lax.ppermute(tail, axis, [(i, (i + 1) % count) for i in range(ends)]),
                cells,
                lax.ppermute(head, axis, [((i + 1) % count, i) for i in range(ends)]),
            ],
            axis=dim,
        )
    return cells


def tables(positions, head_width):
    middle = head_width // 2
    frequency = jnp.exp(
        -(2.0 / head_width) * math.log(THETA) * jnp.arange(middle, dtype=jnp.float32)
    )
    angles = positions.astype(jnp.float32)[:, None] * frequency[None, :]
    angles = jnp.concatenate([angles, angles], axis=1)
    return (jnp.cos(angles), jnp.sin(angles))


def rotate(values, cosine_table, sine_table):
    middle = values.shape[-1] // 2
    turned = jnp.concatenate([-values[..., middle:], values[..., :middle]], axis=-1)
    return values * cosine_table + turned * sine_table


def combine_parts(earlier, later):
    first_max, first_total, first_out = earlier
    second_max, second_total, second_out = later
    overall = jnp.maximum(first_max, second_max)
    first_factor = jnp.exp(first_max - overall)
    second_factor = jnp.exp(second_max - overall)
    return (
        overall,
        first_total * first_factor + second_total * second_factor,
        first_out * first_factor[:, None] + second_out * second_factor[:, None],
    )


def on_device(
    hidden,
    norm_gain,
    query_weight,
    key_weight,
    value_weight,
    output_weight,
    block_reach,
    header_ids,
):
    row_count = hidden.shape[0]
    part_width = hidden.shape[1]
    head_width = key_weight.shape[1]
    local_blocks = row_count // BLOCK
    total_blocks = local_blocks * lax.axis_size("seq")
    seq_place = lax.axis_index("seq")
    floats = hidden.astype(jnp.float32)
    squares = lax.psum(jnp.sum(floats * floats, axis=1), "section")
    scaling = lax.rsqrt(squares / (part_width * lax.axis_size("section")) + EPSILON)
    normed_part = (floats * scaling[:, None] * norm_gain.astype(jnp.float32)[None, :]).astype(
        jnp.bfloat16
    )
    weight_rows = query_weight
    query_sum = jnp.dot(
        lax.all_gather(normed_part, "section", axis=1, tiled=True),
        weight_rows,
        preferred_element_type=jnp.float32,
    )
    key_sum, value_sum = lax.psum(
        (
            jnp.dot(normed_part, key_weight, preferred_element_type=jnp.float32),
            jnp.dot(normed_part, value_weight, preferred_element_type=jnp.float32),
        ),
        "section",
    )
    positions = seq_place * row_count + jnp.arange(row_count, dtype=jnp.int32)
    cosine_table, sine_table = tables(positions, head_width)
    queries = rotate(query_sum, cosine_table, sine_table).astype(jnp.bfloat16)
    keys_here = rotate(key_sum, cosine_table, sine_table).astype(jnp.bfloat16)
    values_here = value_sum.astype(jnp.bfloat16)
    packed = jnp.concatenate([queries, keys_here, values_here], axis=1)
    block_numbers = seq_place * local_blocks + jnp.arange(local_blocks, dtype=jnp.int32)
    select = header_ids[:, None] == block_numbers[None, :]
    shaped = packed.reshape(local_blocks, BLOCK, 3 * head_width)
    picked = jnp.einsum(
        "hb,bre->hre", select.astype(jnp.bfloat16), shaped, preferred_element_type=jnp.float32
    )
    header_pack = lax.psum(picked, "seq").astype(jnp.bfloat16).reshape(-1, 3 * head_width)
    head_queries = header_pack[:, :head_width]
    head_keys = header_pack[:, head_width : 2 * head_width]
    head_values = header_pack[:, 2 * head_width :]
    inverse_root = 1.0 / math.sqrt(head_width)
    far_scores = (
        jnp.einsum("qd,kd->qk", head_queries, keys_here, preferred_element_type=jnp.float32)
        * inverse_root
    )
    far_max = jnp.max(far_scores, axis=1)
    far_weights = jnp.exp(far_scores - far_max[:, None])
    far_total = jnp.sum(far_weights, axis=1)
    far_out = jnp.dot(
        far_weights.astype(jnp.bfloat16), values_here, preferred_element_type=jnp.float32
    )
    merged_max, merged_total, merged_out = merged(
        (far_max, far_total, far_out), "seq", combine_parts
    )
    header_result = merged_out / merged_total[:, None]
    margin_rows = REACH * BLOCK
    stacked = jnp.concatenate([keys_here, values_here], axis=1)
    extended = padded(stacked, (("seq", 0),), margin_rows)
    near_keys = extended[:, :head_width]
    near_values = extended[:, head_width:]
    extent = row_count + 2 * margin_rows
    key_blocks = seq_place * local_blocks - REACH + jnp.arange(extent, dtype=jnp.int32) // BLOCK
    query_blocks = seq_place * local_blocks + jnp.arange(row_count, dtype=jnp.int32) // BLOCK
    limits = jnp.repeat(block_reach, BLOCK)
    key_header = jnp.any(header_ids[:, None] == key_blocks[None, :], axis=0)
    allowed = (key_blocks >= 0)[None, :] & (key_blocks < total_blocks)[None, :]
    allowed = allowed & (jnp.abs(key_blocks[None, :] - query_blocks[:, None]) <= limits[:, None])
    allowed = allowed & jnp.logical_not(key_header)[None, :]
    near_scores = (
        jnp.einsum("qd,kd->qk", queries, near_keys, preferred_element_type=jnp.float32)
        * inverse_root
    )
    near_scores = jnp.where(allowed, near_scores, -jnp.inf)
    head_scores = (
        jnp.einsum("qd,kd->qk", queries, head_keys, preferred_element_type=jnp.float32)
        * inverse_root
    )
    scores = jnp.concatenate([near_scores, head_scores], axis=1)
    row_top = jnp.max(scores, axis=1)
    weights = jnp.exp(scores - row_top[:, None])
    row_sums = jnp.sum(weights, axis=1)
    joined = jnp.concatenate([near_values, head_values], axis=0)
    mixed_out = (
        jnp.dot(weights.astype(jnp.bfloat16), joined, preferred_element_type=jnp.float32)
        / row_sums[:, None]
    )
    header_local = jnp.einsum(
        "hb,hre->bre", select.astype(jnp.float32), header_result.reshape(-1, BLOCK, head_width)
    )
    is_local_header = jnp.any(select, axis=0)
    attended = jnp.where(
        is_local_header[:, None, None],
        header_local,
        mixed_out.reshape(local_blocks, BLOCK, head_width),
    )
    attended = attended.reshape(row_count, head_width).astype(jnp.bfloat16)
    weight_rows = output_weight
    result = jnp.dot(
        lax.all_gather(attended, "section", axis=1, tiled=True),
        weight_rows,
        preferred_element_type=jnp.float32,
    )
    return result.astype(jnp.bfloat16)


def solution(mesh):
    return jax.shard_map(
        on_device,
        mesh=mesh,
        in_specs=(
            P("seq", "section"),
            P("section"),
            P(None, "section"),
            P("section", None),
            P("section", None),
            P(None, "section"),
            P("seq"),
            P(),
        ),
        out_specs=P("seq", "section"),
        check_vma=False,
    )
```

profile of v0, /device:TPU:64, one launch (start us, length us, event | category | flops | bytes accessed | tf_op | source)
XLA Modules:
  0.0 913.6 jit_solution(16988144689448362159)
XLA Ops:
  7.3 1.5 fusion.2
  8.8 10.5 %psum.28 = f32[512]{0:T(512)S(1)} all-reduce(f32[512]{0:T(512)S(1)} %fusion.2), channel_id=1, replica_groups=mesh['section'=4,'seq'=128] {'section'}, use_global_device_ids=true, to_apply=%region_2.0 | all-reduce | flops 512 | bytes 4096 | tf_op jit(solution)/shard_map/psum | solution.py:86
  19.3 1.6 fusion.4
  20.9 1.2 fusion.53
  23.0 1.7 fusion.54
  24.8 17.2 %all-reduce.5 = bf16[512,128]{0,1:T(8,128)(2,1)S(1)} all-reduce(f32[512,128]{0,1:T(8,128)S(1)} %fusion.54), channel_id=1, replica_groups=mesh['section'=4,'seq'=128] {'section'}, use_global_device_ids=true, to_apply=%region_4.0 | all-reduce | flops 65536 | bytes 393216 | tf_op jit(solution)/shard_map/psum | solution.py:97
  42.0 34.5 %all-reduce.4.cloned.1.call-done = f32[512,128]{0,1:T(8,128)} async-done(((f32[512,128]{0,1:T(8,128)}), f32[512,128]{0,1:T(8,128)}) %all-reduce.4.cloned.1.call-update) | async-done | bytes 262160 | tf_op jit(solution)/shard_map/psum | solution.py:97
  77.5 55.5 %all-gather.8.cloned.1.call-done = bf16[512,4096]{1,0:T(8,128)(2,1)} async-done(((bf16[512,1024]{1,0:T(8,128)(2,1)}), bf16[512,4096]{1,0:T(8,128)(2,1)}) %all-gather.8.cloned.1.call-update) | async-done | bytes 4194320 | tf_op jit(solution)/shard_map/all_gather | solution.py:93
  133.0 3.7 fusion.52
  138.7 461.0 %all-reduce.6 = bf16[2,128,384]{2,0,1:T(2,128)(2,1)S(1)} all-reduce(f32[2,128,384]{2,0,1:T(2,128)S(1)} %fusion.48), channel_id=1, replica_groups=mesh['section'=4,'seq'=128] {'seq'}, use_global_device_ids=true, to_apply=%region_5.0 | all-reduce | flops 98304 | bytes 589824 | tf_op jit(solution)/shard_map/psum | solution.py:116
  601.6 82.4 %all-gather.3 = f32[128,1,256]{2,1,0:T(1,128)S(1)} all-gather(f32[1,1,256]{2,1,0:T(1,128)S(1)} %bitcast.66), channel_id=2, replica_groups=mesh['section'=4,'seq'=128] {'seq'}, dimensions={0}, use_global_device_ids=true | all-gather | bytes 132096 | tf_op jit(solution)/shard_map/all_gather | solution.py:14
  684.3 47.1 %all-gather.4 = f32[128,1,256]{2,1,0:T(1,128)S(1)} all-gather(f32[1,1,256]{2,1,0:T(1,128)S(1)} %bitcast.67), channel_id=3, replica_groups=mesh['section'=4,'seq'=128] {'seq'}, dimensions={0}, use_global_device_ids=true | all-gather | bytes 132096 | tf_op jit(solution)/shard_map/all_gather | solution.py:14
  731.4 4.6 collective-permute-start.1
  736.0 1.9 collective-permute-start
  738.5 5.9 collective-permute-done
  748.1 144.2 %while.19 = (s32[]{:T(128)}, f32[256]{0:T(256)S(1)}, f32[256]{0:T(256)S(1)}, f32[256,128]{1,0:T(8,128)S(1)}, f32[128,256]{1,0:T(8,128)S(1)}, /*index=5*/f32[128,...) while((s32[]{:T(128)}, f32[256]{0:T(256)S(1)}, f32[256]{0:T(256)S(1)}, ...), condition=%wide.region_9.10_spmd, body=%wide.region_8.0_spmd.sunk | while | flops 99845 | bytes 407703 | solution.py:20
  749.3 1.1 fusion.69
  751.5 1.1 fusion.69
  753.8 1.1 fusion.69
  754.9 1.1 fusion.69
  756.1 1.1 fusion.69
  757.2 1.1 fusion.69
  758.3 1.1 fusion.69
  759.5 1.1 fusion.69
  761.7 1.1 fusion.69
  764.0 1.1 fusion.69
  766.3 1.1 fusion.69
  768.6 1.1 fusion.69
  770.8 1.1 fusion.69
  773.1 1.1 fusion.69
  775.4 1.1 fusion.69
  776.5 1.1 fusion.69
  777.6 1.1 fusion.69
  778.8 1.1 fusion.69
  779.9 1.1 fusion.69
  781.1 1.1 fusion.69
  783.3 1.1 fusion.69
  785.6 1.1 fusion.69
  787.9 1.1 fusion.69
  790.1 1.1 fusion.69
  792.4 1.1 fusion.69
  794.7 1.1 fusion.69
  797.0 1.1 fusion.69
  798.1 1.1 fusion.69
  799.2 1.1 fusion.69
  800.4 1.1 fusion.69
  801.5 1.1 fusion.69
  802.6 1.1 fusion.69
  804.9 1.1 fusion.69
  807.2 1.1 fusion.69
  809.4 1.1 fusion.69
  811.7 1.1 fusion.69
  814.0 1.1 fusion.69
  816.3 1.1 fusion.69
  818.5 1.1 fusion.69
  819.7 1.1 fusion.69
  820.8 1.1 fusion.69
  821.9 1.1 fusion.69
  823.1 1.1 fusion.69
  824.2 1.1 fusion.69
  826.5 1.1 fusion.69
  828.8 1.1 fusion.69
  892.8 12.6 %all_gather.31 = bf16[512,512]{1,0:T(8,128)(2,1)S(1)} all-gather(bf16[512,128]{1,0:T(8,128)(2,1)S(1)} %bitcast.59), channel_id=1, replica_groups=mesh['section'=4,'seq'=128] {'section'}, dimensions={1}, use_global_device_ids=true | all-gather | bytes 655360 | tf_op jit(solution)/shard_map/all_gather | solution.py:178
  905.4 1.7 convolution_convert_fusion
  (410 shorter events, 102.1 us)
Async XLA Ops:
  6.5 898.9 %copy-start = (bf16[512,1024]{1,0:T(8,128)(2,1)S(1)}, bf16[512,1024]{1,0:T(8,128)(2,1)}, u32[]{:S(2)}) copy-start(bf16[512,1024]{1,0:T(8,128)(2,1)} %param.15) | copy-start | bytes 3145732
  6.5 14.4 %copy-start.7 = (bf16[1024,128]{1,0:T(8,128)(2,1)S(1)}, bf16[1024,128]{1,0:T(8,128)(2,1)}, u32[]{:S(2)}) copy-start(bf16[1024,128]{1,0:T(8,128)(2,1)} %param.13) | copy-start | bytes 786436
  6.5 70.0 %all-reduce.4.cloned.1.call-start = ((), (), s32[]{:S(2)}) async-start(), calls=%async_computation.1 | async-start | bytes 524288 | tf_op jit(solution)/shard_map/psum | solution.py:97
  19.3 3.6 copy-start.8
  20.9 1.3 copy-start.1
  22.1 110.9 %copy-start.4 = (bf16[4096,128]{1,0:T(8,128)(2,1)S(1)}, bf16[4096,128]{1,0:T(8,128)(2,1)}, u32[]{:S(2)}) copy-start(bf16[4096,128]{1,0:T(8,128)(2,1)} %param.12) | copy-start | bytes 3145732
  22.2 110.8 %all-gather.8.cloned.1.call-start = ((), (), s32[]{:S(2)}) async-start(), calls=%async_computation | async-start | bytes 5242880 | tf_op jit(solution)/shard_map/all_gather | solution.py:93
  22.9 724.2 %all-gather.10.cloned.1.call-start = ((), (), s32[]{:S(2)}) async-start(), calls=%async_computation.2 | async-start | bytes 16908288 | tf_op jit(solution)/shard_map/all_gather | solution.py:14
  77.5 59.2 %copy-start.3 = (f32[512,128]{0,1:T(8,128)S(1)}, f32[512,128]{0,1:T(8,128)}, u32[]{:S(2)}) copy-start(f32[512,128]{0,1:T(8,128)} %all-reduce.4.cloned.1.call-done) | copy-start | bytes 786436
  136.7 1.6 copy-start.9
  138.3 463.3 %copy-start.10 = (s32[4]{0:T(128)S(1)}, s32[4]{0:T(128)}, u32[]{:S(2)}) copy-start(s32[4]{0:T(128)} %param.16) | copy-start | bytes 52
  684.1 61.5 %copy-start.6 = (f32[128,1,256]{2,1,0:T(1,128)}, f32[128,1,256]{2,1,0:T(1,128)S(1)}, u32[]{:S(2)}) copy-start(f32[128,1,256]{2,1,0:T(1,128)S(1)} %all-gather.3) | copy-start | bytes 393220
  731.4 14.1 %copy-start.5 = (f32[128,1,256]{2,1,0:T(1,128)}, f32[128,1,256]{2,1,0:T(1,128)S(1)}, u32[]{:S(2)}) copy-start(f32[128,1,256]{2,1,0:T(1,128)S(1)} %all-gather.4) | copy-start | bytes 393220
  731.4 7.1 collective-permute-start.1
  736.0 8.4 collective-permute-start
  744.5 1.1 copy-start.2
  745.6 1.0 slice-start
  746.5 1.5 slice-start.1
  746.5 1.5 slice-start.2
Sparse Core Ops, SparseCore 0:
  22.3 54.2 all-reduce.3
  78.9 54.1 all-gather.7
  601.4 126.7 all-gather.9
where the time goes:
time: 916 us; the launch traced here: 914 us
  blocking collectives  631 us (69%)
  other arithmetic  146 us (16%)
  waiting for transfers between devices  96.8 us (11%)
  between operations  13.5 us (1%)
  matrix products  12.3 us (1%)
    psum x1, blocking collectives, on_device(): lax.psum(picked, 'seq').astype(jnp.bfloat16).reshape(-1, 3 * head_width)  461 us
    add x127, other arithmetic, combine_parts(): first_out * first_factor[:, None] + second_out * second_factor[:, None]  136 us
    all_gather x2, blocking collectives, merged(): everything = jax.tree.map(lambda part: lax.all_gather(part, axis), value)  130 us
    all_gather x1, waiting for transfers between devices, on_device(): lax.all_gather(normed_part, 'section', axis=1, tiled=True)  55.5 us
    psum x1, waiting for transfers between devices, on_device(): lax.psum((jnp.dot(normed_part, key_weight, preferred_element_type=jnp.flo...  34.5 us
  transfers between devices with their start and end apart: 5, of which 4 were waited for; matrix products, arithmetic and copies ran while one was open for 1% of the time, Pallas kernels for 0%

commit v1 on v0

--- a/solution.py
+++ b/solution.py
@@ -90,7 +90,10 @@
     )
     weight_rows = query_weight
     query_sum = jnp.dot(
-        lax.all_gather(normed_part, "section", axis=1, tiled=True),
+        jnp.concatenate(
+            lax.all_to_all(jnp.stack([normed_part] * lax.axis_size("section")), "section", 0, 0),
+            axis=1,
+        ),
         weight_rows,
         preferred_element_type=jnp.float32,
     )

time: 916 us -> 887 us (0.968)
  waiting for transfers between devices: 96.8 us -> 20.9 us
  blocking collectives: 631 us -> 671 us
    all_gather x1 -> x0, waiting for transfers between devices: 55.5 us -> none  [on_device(): lax.all_gather(normed_part, 'section', axis=1, tiled=True)]
    psum x1, blocking collectives: 17.2 us -> 59.8 us  [on_device(): lax.psum((jnp.dot(normed_part, key_weight, preferred_element_type=jnp.flo...]
    psum x1, waiting for transfers between devices: 34.5 us -> 14.8 us  [on_device(): lax.psum((jnp.dot(normed_part, key_weight, preferred_element_type=jnp.flo...]
  transfers between devices with their start and end apart: 5 -> 5, of which waited for: 4 -> 3; matrix products, arithmetic and copies ran while one was open for 1% -> 1% of each run, Pallas kernels for 0% -> 0%
where the time goes in v1:
time: 887 us; the launch traced here: 885 us
  blocking collectives  671 us (76%)
  other arithmetic  146 us (16%)
  waiting for transfers between devices  20.9 us (2%)
  between operations  13.8 us (2%)
  starting transfers between devices  11.5 us (1%)
  matrix products  10.7 us (1%)
    psum x1, blocking collectives, on_device(): lax.psum(picked, 'seq').astype(jnp.bfloat16).reshape(-1, 3 * head_width)  459 us
    add x127, other arithmetic, combine_parts(): first_out * first_factor[:, None] + second_out * second_factor[:, None]  136 us
    all_gather x2, blocking collectives, merged(): everything = jax.tree.map(lambda part: lax.all_gather(part, axis), value)  130 us
    psum x1, blocking collectives, on_device(): lax.psum((jnp.dot(normed_part, key_weight, preferred_element_type=jnp.flo...  59.8 us
  transfers between devices with their start and end apart: 5, of which 3 were waited for; matrix products, arithmetic and copies ran while one was open for 1% of the time, Pallas kernels for 0%

profile of v1, /device:TPU:64, one launch (start us, length us, event | category | flops | bytes accessed | tf_op | source)
XLA Modules:
  0.0 884.7 jit_solution(12834288926780357710)
XLA Ops:
  7.3 1.5 fusion.2
  8.8 10.5 %psum.28 = f32[512]{0:T(512)S(1)} all-reduce(f32[512]{0:T(512)S(1)} %fusion.2), channel_id=1, replica_groups=mesh['section'=4,'seq'=128] {'section'}, use_global_device_ids=true, to_apply=%region_2.0 | all-reduce | flops 512 | bytes 4096 | tf_op jit(solution)/shard_map/psum | solution.py:86
  19.3 1.5 fusion.4
  21.4 2.3 stack.2
  23.7 5.0 all-to-all-start
  28.8 1.2 fusion.53
  30.7 59.8 %all-reduce.5 = bf16[512,128]{0,1:T(8,128)(2,1)S(1)} all-reduce(f32[512,128]{0,1:T(8,128)S(1)} %fusion.54), channel_id=1, replica_groups=mesh['section'=4,'seq'=128] {'section'}, use_global_device_ids=true, to_apply=%region_4.0 | all-reduce | flops 65536 | bytes 393216 | tf_op jit(solution)/shard_map/psum | solution.py:100
  90.5 14.8 %all-reduce.4.cloned.1.call-done = f32[512,128]{0,1:T(8,128)} async-done(((f32[512,128]{0,1:T(8,128)}), f32[512,128]{0,1:T(8,128)}) %all-reduce.4.cloned.1.call-update) | async-done | bytes 262160 | tf_op jit(solution)/shard_map/psum | solution.py:100
  106.3 3.3 fusion.52
  111.6 458.9 %all-reduce.6 = bf16[2,128,384]{2,0,1:T(2,128)(2,1)S(1)} all-reduce(f32[2,128,384]{2,0,1:T(2,128)S(1)} %fusion.48), channel_id=1, replica_groups=mesh['section'=4,'seq'=128] {'seq'}, use_global_device_ids=true, to_apply=%region_5.0 | all-reduce | flops 98304 | bytes 589824 | tf_op jit(solution)/shard_map/psum | solution.py:119
  572.4 82.4 %all-gather.3 = f32[128,1,256]{2,1,0:T(1,128)S(1)} all-gather(f32[1,1,256]{2,1,0:T(1,128)S(1)} %bitcast.69), channel_id=2, replica_groups=mesh['section'=4,'seq'=128] {'seq'}, dimensions={0}, use_global_device_ids=true | all-gather | bytes 132096 | tf_op jit(solution)/shard_map/all_gather | solution.py:14
  655.1 47.1 %all-gather.4 = f32[128,1,256]{2,1,0:T(1,128)S(1)} all-gather(f32[1,1,256]{2,1,0:T(1,128)S(1)} %bitcast.70), channel_id=3, replica_groups=mesh['section'=4,'seq'=128] {'seq'}, dimensions={0}, use_global_device_ids=true | all-gather | bytes 132096 | tf_op jit(solution)/shard_map/all_gather | solution.py:14
  702.2 4.5 collective-permute-start.1
  706.8 1.9 collective-permute-start
  709.3 5.9 collective-permute-done
  718.8 144.2 %while.19 = (s32[]{:T(128)}, f32[256]{0:T(256)S(1)}, f32[256]{0:T(256)S(1)}, f32[256,128]{1,0:T(8,128)S(1)}, f32[128,256]{1,0:T(8,128)S(1)}, /*index=5*/f32[128,...) while((s32[]{:T(128)}, f32[256]{0:T(256)S(1)}, f32[256]{0:T(256)S(1)}, ...), condition=%wide.region_9.10_spmd, body=%wide.region_8.0_spmd.sunk | while | flops 99845 | bytes 407703 | solution.py:20
  720.0 1.1 fusion.69
  721.1 1.1 fusion.69
  722.3 1.1 fusion.69
  723.4 1.1 fusion.69
  724.5 1.1 fusion.69
  725.7 1.1 fusion.69
  727.9 1.1 fusion.69
  730.2 1.1 fusion.69
  732.5 1.1 fusion.69
  734.8 1.1 fusion.69
  737.0 1.1 fusion.69
  739.3 1.1 fusion.69
  741.6 1.1 fusion.69
  742.7 1.1 fusion.69
  743.8 1.1 fusion.69
  745.0 1.1 fusion.69
  746.1 1.1 fusion.69
  747.2 1.1 fusion.69
  749.5 1.1 fusion.69
  751.8 1.1 fusion.69
  754.1 1.1 fusion.69
  756.3 1.1 fusion.69
  758.6 1.1 fusion.69
  760.9 1.1 fusion.69
  763.1 1.1 fusion.69
  764.3 1.1 fusion.69
  765.4 1.1 fusion.69
  766.6 1.1 fusion.69
  767.7 1.1 fusion.69
  768.8 1.1 fusion.69
  771.1 1.1 fusion.69
  773.4 1.1 fusion.69
  775.6 1.1 fusion.69
  777.9 1.1 fusion.69
  780.2 1.1 fusion.69
  782.5 1.1 fusion.69
  784.7 1.1 fusion.69
  785.9 1.1 fusion.69
  787.0 1.1 fusion.69
  788.1 1.1 fusion.69
  789.3 1.1 fusion.69
  790.4 1.1 fusion.69
  792.7 1.1 fusion.69
  794.9 1.1 fusion.69
  797.2 1.1 fusion.69
  799.5 1.1 fusion.69
  863.5 12.7 %all_gather.27 = bf16[512,512]{1,0:T(8,128)(2,1)S(1)} all-gather(bf16[512,128]{1,0:T(8,128)(2,1)S(1)} %bitcast.62), channel_id=1, replica_groups=mesh['section'=4,'seq'=128] {'section'}, dimensions={1}, use_global_device_ids=true | all-gather | bytes 655360 | tf_op jit(solution)/shard_map/all_gather | solution.py:181
  876.2 1.7 convolution_convert_fusion
  (407 shorter events, 102.4 us)
Async XLA Ops:
  6.5 869.7 %copy-start = (bf16[512,1024]{1,0:T(8,128)(2,1)S(1)}, bf16[512,1024]{1,0:T(8,128)(2,1)}, u32[]{:S(2)}) copy-start(bf16[512,1024]{1,0:T(8,128)(2,1)} %param.15) | copy-start | bytes 3145732
  23.7 5.1 copy-start.5
  23.7 6.3 copy-start.6
  23.7 82.5 %all-to-all-start = ((bf16[4,512,1024]{1,2,0:T(8,128)(2,1)}), bf16[4,512,1024]{1,2,0:T(8,128)(2,1)}, u32[]{:S(2)}, u32[]{:S(2)}) async-start(bf16[4,512,1024]{1,2,0:T(8,128)(2,1)} %stack.2), calls=%async_computation | async-start | bytes 8388608 | tf_op jit(solution)/shard_map/all_to_all | solution.py:94
  28.7 76.5 %all-reduce.4.cloned.1.call-start = ((), (), s32[]{:S(2)}) async-start(), calls=%async_computation.1 | async-start | bytes 524288 | tf_op jit(solution)/shard_map/psum | solution.py:100
  30.0 687.9 %all-gather.7.cloned.1.call-start = ((), (), s32[]{:S(2)}) async-start(), calls=%async_computation.2 | async-start | bytes 16908288 | tf_op jit(solution)/shard_map/all_gather | solution.py:14
  106.2 3.4 copy-start.2
  109.6 1.6 copy-start.7
  111.2 461.2 %copy-start.8 = (s32[4]{0:T(128)S(1)}, s32[4]{0:T(128)}, u32[]{:S(2)}) copy-start(s32[4]{0:T(128)} %param.16) | copy-start | bytes 52
  654.8 61.4 %copy-start.4 = (f32[128,1,256]{2,1,0:T(1,128)}, f32[128,1,256]{2,1,0:T(1,128)S(1)}, u32[]{:S(2)}) copy-start(f32[128,1,256]{2,1,0:T(1,128)S(1)} %all-gather.3) | copy-start | bytes 393220
  702.2 14.1 %copy-start.3 = (f32[128,1,256]{2,1,0:T(1,128)}, f32[128,1,256]{2,1,0:T(1,128)S(1)}, u32[]{:S(2)}) copy-start(f32[128,1,256]{2,1,0:T(1,128)S(1)} %all-gather.4) | copy-start | bytes 393220
  702.2 7.0 collective-permute-start.1
  706.8 8.4 collective-permute-start
  715.2 1.1 copy-start.1
  716.3 1.0 slice-start
  717.2 1.5 slice-start.1
  717.2 1.5 slice-start.2
Sparse Core Ops, SparseCore 0:
  31.9 73.3 all-reduce.3
  572.2 127.0 all-gather.6
